TPU v7x, 512 devices: a whole 4x8x8 slice. The times are simulated.
512 devices in a mesh: dp: 16 (over z, core), latent: 32 (over x, y).
Axes of the slice: x: 4, y: 8, z: 8, core: 2. Of those that a mesh axis runs over, the one named last changes fastest.
Arguments:
- activations: bfloat16 [16384, 8192], P('latent', 'dp'), may hold values from -6 to 6
- weight: bfloat16 [8192, 8192], P('dp', 'latent'), may hold values from -0.0625 to 0.0625
- enc_bias: float32 [8192], replicated, may hold values from -3 to 3
- dec_bias: float32 [8192], P('dp'), may hold values from -3 to 3
- block_ids: int32 [32, 8], P('latent'), may hold values from 0 to 63, as said below
- counts: int32 [32], P('latent'), may hold values from 1 to 8, as said below
Outputs:
- weight_grad: float32 [8192, 8192], P('dp', 'latent')
- row_error: float32 [16384], P(('latent', 'dp'))
Inputs may be any that keep to these rules, and one draw needn't show every extreme that they name: `block_ids`: each row block's list names 8 latent blocks of 8 different owners (block k belongs to owner k // 2); only its first counts entries are active, and some blocks are listed far more often than others. `counts`: some row block has all 8 entries active.
All inputs are finite; a program needn't handle non-finite values.
Results may differ from a plain program's by a relative error of at most 0.0028.
Values may be sent and summed in bfloat16 or wider, within the bound.
No kernel may reach another device: no remote copies, remote signals or barrier semaphores. Data moves between devices by JAX's collectives and lax.ppermute only.
A program may use at most 64 MiB of HBM per device.

v0:
```python
import math
import jax
import jax.numpy as jnp
from jax import lax
from jax.sharding import PartitionSpec as P

BLK = 128


def on_device(activations, weight, enc_bias, dec_bias, block_ids, counts):
    rows, width = activations.shape
    block = BLK
    per_owner = weight.shape[1] // block
    owners = lax.axis_size("latent")
    groups = lax.axis_size("dp")
    share = rows // groups
    myself = lax.axis_index("latent")
    all_ids, all_counts = (
        lax.all_gather(block_ids, "latent", axis=0, tiled=True),
        lax.all_gather(counts, "latent", axis=0, tiled=True),
    )
    ids = block_ids[0]
    slots = ids.shape[0]
    live = (jnp.arange(slots) < counts[0]).astype(jnp.float32)
    live_cols = live[:, None, None]
    all_live = (jnp.arange(slots)[None, :] < all_counts[:, None]).astype(jnp.float32)
    own_blocks = myself * per_owner + jnp.arange(per_owner)
    matches = (all_ids[:, :, None] == own_blocks[None, None, :]).astype(jnp.float32) * all_live[
        :, :, None
    ]
    selection = jnp.sum(matches, axis=1).astype(jnp.bfloat16)
    source = (
        (ids[:, None] // per_owner == jnp.arange(owners)[None, :]).astype(jnp.float32)
        * live[:, None]
    ).astype(jnp.bfloat16)
    scale_grad = 2.0 / math.sqrt(rows * owners)
    centered = (activations.astype(jnp.float32) - dec_bias).astype(jnp.bfloat16)
    piece = lax.all_gather(weight, "latent", axis=1, tiled=True)
    number = piece.shape[1] // block
    wanted = (ids[:, None] == jnp.arange(number)[None, :]).astype(jnp.bfloat16)
    picked = jnp.einsum(
        "sb,dbk->sdk",
        wanted,
        piece.reshape(width, number, block),
        preferred_element_type=jnp.float32,
    )
    tiles = picked.astype(jnp.bfloat16)
    bias_rows = jnp.take(enc_bias.reshape(-1, block), ids, axis=0)[:, None, :]
    part_pre = jnp.einsum("rd,sdk->srk", centered, tiles, preferred_element_type=jnp.float32)
    pre = lax.psum(part_pre, "dp") + bias_rows
    act = (jnp.maximum(pre, 0.0) * live_cols).astype(jnp.bfloat16)
    recon = jnp.einsum("srk,sdk->rd", act, tiles, preferred_element_type=jnp.float32) + dec_bias
    err = recon - activations.astype(jnp.float32)
    grad_out = (err * scale_grad).astype(jnp.bfloat16)
    part_loss = jnp.sum(err * err, axis=1) / (width * groups)
    part_grad = jnp.einsum("rd,sdk->srk", grad_out, tiles, preferred_element_type=jnp.float32)
    grad_act, row_total = lax.psum((part_grad, part_loss), "dp")
    grad_pre = (jnp.where(pre > 0, grad_act, 0.0) * live_cols).astype(jnp.bfloat16)
    row_error = lax.dynamic_slice_in_dim(row_total, lax.axis_index("dp") * share, share)
    first = jnp.einsum("rd,srk->sdk", centered, grad_pre, preferred_element_type=jnp.float32)
    second = jnp.einsum("rd,srk->sdk", grad_out, act, preferred_element_type=jnp.float32)
    contribution = (first + second).astype(jnp.bfloat16)
    sending = jnp.einsum(
        "sj,sdk->jdk", source, contribution, preferred_element_type=jnp.float32
    ).astype(jnp.bfloat16)
    received = lax.all_to_all(sending, "latent", split_axis=0, concat_axis=0, tiled=True)
    weight_grad = jnp.einsum("rb,rdk->dbk", selection, received, preferred_element_type=jnp.float32)
    return (weight_grad.reshape(width, per_owner * block), row_error)


def solution(mesh):
    placed = (P("latent", "dp"), P("dp", "latent"), P(), P("dp"), P("latent", None), P("latent"))
    return jax.shard_map(
        on_device,
        mesh=mesh,
        in_specs=placed,
        out_specs=(P("dp", "latent"), P(("latent", "dp"))),
        check_vma=False,
    )
```

profile of v0, /device:TPU:1, one launch (start us, length us, event | category | flops | bytes accessed | tf_op | source)
XLA Modules:
  0.0 583.5 jit_solution(1190068990571921230)
XLA Ops:
  7.2 0.0 copy-start
  7.2 0.0 all-gather.3.cloned.1.call-start
  7.2 0.7 all-gather.3.cloned.1.call-update
  7.9 0.0 all-reduce.4.cloned.1.call-start
  8.0 1.3 copy.19
  9.2 113.8 %all-gather.3.cloned.1.call-done = bf16[512,8192]{1,0:T(8,128)(2,1)} async-done(((bf16[512,256]{1,0:T(8,128)(2,1)}), bf16[512,8192]{1,0:T(8,128)(2,1)}) %all-gather.3.cloned.1.call-update) | async-done | bytes 8388624 | tf_op jit(solution)/shard_map/all_gather | solution.py:38
  123.0 0.0 copy-start.5
  123.0 9.3 %copy.41 = bf16[64,8,64,128]{3,2,1,0:T(8,128)(2,1)} copy(bf16[64,8,64,128]{3,1,2,0:T(8,128)(2,1)} %bitcast.55) | data formatting | bytes 16777216
  132.3 0.0 copy-done.5
  132.3 0.0 copy-start.4
  132.3 4.6 convolution_convert_fusion.1
  136.9 0.0 copy-done.4
  136.9 2.1 convolution_bitcast_fusion.1
  139.1 0.0 all-reduce.4.cloned.1.call-update
  139.1 0.0 all-reduce.6.cloned.1.call-start
  139.8 0.0 copy-done
  139.8 0.6 gather_fusion
  140.4 0.1 broadcast_select_fusion
  140.5 120.1 %all-reduce.4.cloned.1.call-done = f32[8,512,128]{1,2,0:T(8,128)} async-done(((f32[8,512,128]{1,2,0:T(8,128)}), f32[8,512,128]{1,2,0:T(8,128)}) %all-reduce.4.cloned.1.call-update) | async-done | bytes 2097168 | tf_op jit(solution)/shard_map/psum | solution.py:50
  260.6 2.5 multiply_reduce_fusion
  263.1 0.0 copy-start.2
  263.1 1.0 copy-done.2
  264.1 2.1 convolution_bitcast_fusion
  266.1 0.0 copy-start.1
  266.1 0.0 all-reduce.6.cloned.1.call-update
  266.2 120.7 %all-reduce.6.cloned.1.call-done = f32[8,512,128]{1,2,0:T(8,128)} async-done(((f32[8,512,128]{1,2,0:T(8,128)}), f32[8,512,128]{1,2,0:T(8,128)}) %all-reduce.6.cloned.1.call-update) | async-done | bytes 2097168 | tf_op jit(solution)/shard_map/psum | solution.py:57
  386.9 0.0 copy-done.1
  386.9 0.0 copy-start.3
  386.9 2.5 fusion.5
  389.4 0.0 copy-done.3
  389.4 0.8 fusion.2
  390.3 0.8 copy.28
  391.0 1.3 convolution_convert_fusion
  392.4 3.6 copy.29
  396.0 9.4 %all-to-all-start = ((bf16[32,512,128]{2,1,0:T(8,128)(2,1)}), bf16[32,512,128]{2,1,0:T(8,128)(2,1)}, u32[]{:S(2)}, u32[]{:S(2)}) async-start(bf16[32,512,128]{2,1,0:T(8,128)(2,1)} %copy.29), calls=%async_computation | async-start | bytes 8388608 | tf_op jit(solution)/shard_map/all_to_all | solution.py:66
  405.4 116.0 %all-gather = s32[32,1,8]{2,1,0:T(1,128)S(1)} all-gather(s32[1,1,8]{2,1,0:T(1,128)S(1)} %bitcast.60), channel_id=1, replica_groups=mesh['dp'=16,'latent'=32] {'latent'}, dimensions={0}, use_global_device_ids=true | all-gather | bytes 1056 | tf_op jit(solution)/shard_map/all_gather | solution.py:19
  521.4 0.1 copy.30
  521.5 1.3 dynamic-slice
  522.7 0.8 dynamic-update-slice
  523.5 12.8 %all-reduce = s32[32]{0:T(128)S(1)} all-reduce(s32[32]{0:T(128)S(1)} %dynamic-update-slice), channel_id=1, replica_groups=mesh['dp'=16,'latent'=32] {'latent'}, use_global_device_ids=true, to_apply=%add | all-reduce | flops 32 | bytes 256
  536.3 0.1 select_reduce_fusion
  536.4 34.6 %psum.23 = f32[512]{0:T(512)S(1)} all-reduce(f32[512]{0:T(512)S(1)} %broadcast_multiply_fusion), channel_id=1, replica_groups=mesh['dp'=16,'latent'=32] {'dp'}, use_global_device_ids=true, to_apply=%region_4.5 | all-reduce | flops 512 | bytes 4096 | tf_op jit(solution)/shard_map/psum | solution.py:57
  571.0 0.6 dynamic_slice.3
  571.6 0.0 all-to-all-done
  571.6 4.6 fusion
  576.2 0.8 copy.54
  (9 shorter events, 0.0 us)
Async XLA Ops:
  7.2 132.6 %copy-start = (f32[8192]{0:T(1024)S(1)}, f32[8192]{0:T(1024)}, u32[]{:S(2)}) copy-start(f32[8192]{0:T(1024)} %param.8) | copy-start | bytes 98308
  7.2 115.8 %all-gather.3.cloned.1.call-start = ((), (), s32[]{:S(2)}) async-start(), calls=%async_computation.1 | async-start | bytes 8650752 | tf_op jit(solution)/shard_map/all_gather | solution.py:38
  7.9 252.7 %all-reduce.4.cloned.1.call-start = ((), (), s32[]{:S(2)}) async-start(), calls=%async_computation.2 | async-start | bytes 4194304 | tf_op jit(solution)/shard_map/psum | solution.py:50
  123.0 9.3 %copy-start.5 = (s32[1,8]{1,0:T(1,128)S(1)}, s32[1,8]{1,0:T(1,128)}, u32[]{:S(2)}) copy-start(s32[1,8]{1,0:T(1,128)} %param.10) | copy-start | bytes 100
  132.3 4.6 copy-start.4
  139.1 247.8 %all-reduce.6.cloned.1.call-start = ((), (), s32[]{:S(2)}) async-start(), calls=%async_computation.3 | async-start | bytes 4194304 | tf_op jit(solution)/shard_map/psum | solution.py:57
  263.1 1.0 copy-start.2
  266.1 120.8 %copy-start.1 = (f32[8,512,128]{1,2,0:T(8,128)S(1)}, f32[8,512,128]{1,2,0:T(8,128)}, u32[]{:S(2)}) copy-start(f32[8,512,128]{1,2,0:T(8,128)} %all-reduce.4.cloned.1.call-done) | copy-start | bytes 6291460
  386.9 2.6 copy-start.3
  396.0 175.6 %all-to-all-start = ((bf16[32,512,128]{2,1,0:T(8,128)(2,1)}), bf16[32,512,128]{2,1,0:T(8,128)(2,1)}, u32[]{:S(2)}, u32[]{:S(2)}) async-start(bf16[32,512,128]{2,1,0:T(8,128)(2,1)} %copy.29), calls=%async_computation | async-start | bytes 8388608 | tf_op jit(solution)/shard_map/all_to_all | solution.py:66
Sparse Core Ops, SparseCore 0:
  11.1 111.8 all-gather.2
  139.2 121.3 all-reduce.3
  266.3 120.5 all-reduce.5
where the time goes:
time: 584 us
  waiting for transfers between devices  355 us (61%)
  blocking collectives  163 us (28%)
  matrix products  20.6 us (4%)
  local copies, waits for them, and re-layouts  20 us (3%)
  between operations  14.5 us (2%)
  starting transfers between devices  9.52 us (2%)
    psum x1, waiting for transfers between devices, on_device(): grad_act, row_total = lax.psum((part_grad, part_loss), 'dp')  121 us
    psum x1, waiting for transfers between devices, on_device(): pre = lax.psum(part_pre, 'dp') + bias_rows  120 us
    all_gather x1, blocking collectives, on_device(): lax.all_gather(block_ids, 'latent', axis=0, tiled=True)  116 us
    all_gather x1, waiting for transfers between devices, on_device(): piece = lax.all_gather(weight, 'latent', axis=1, tiled=True)  114 us
    psum x1, blocking collectives, on_device(): grad_act, row_total = lax.psum((part_grad, part_loss), 'dp')  34.6 us
    unnamed x19, local copies, waits for them, and re-layouts  14.5 us
    unnamed x1, blocking collectives  12.8 us
  transfers between devices with their start and end apart: 4, of which 3 were waited for; matrix products, arithmetic and copies ran while one was open for 1% of the time, Pallas kernels for 0%

commit v1 on v0

--- a/solution.py
+++ b/solution.py
@@ -5,6 +5,13 @@
 from jax.sharding import PartitionSpec as P
 
 BLK = 128
+
+
+def exchange_gather(array, axis, dim):
+    size = lax.axis_size(axis)
+    blocks = jnp.stack([array for _ in range(size)])
+    blocks = lax.all_to_all(blocks, axis, split_axis=0, concat_axis=0)
+    return jnp.concatenate(blocks, axis=dim)
 
 
 def on_device(activations, weight, enc_bias, dec_bias, block_ids, counts):
@@ -16,7 +23,7 @@
     share = rows // groups
     myself = lax.axis_index("latent")
     all_ids, all_counts = (
-        lax.all_gather(block_ids, "latent", axis=0, tiled=True),
+        exchange_gather(block_ids, "latent", 0),
         lax.all_gather(counts, "latent", axis=0, tiled=True),
     )
     ids = block_ids[0]

time: 584 us -> 551 us (0.943)
  blocking collectives: 163 us -> 130 us
  waiting for transfers between devices: 355 us -> 345 us
  starting transfers between devices: 9.52 us -> 18.8 us
    all_gather x1 -> x0, blocking collectives: 116 us -> none  [on_device(): lax.all_gather(block_ids, 'latent', axis=0, tiled=True)]
    unnamed x1, blocking collectives: 12.8 us -> 103 us
    psum x1, waiting for transfers between devices: 121 us -> 111 us  [on_device(): grad_act, row_total = lax.psum((part_grad, part_loss), 'dp')]
    all_to_all x0 -> x1, starting transfers between devices: none -> 9.26 us  [exchange_gather(): blocks = lax.all_to_all(blocks, axis, split_axis=0, concat_axis=0)]
    psum x1, blocking collectives: 34.6 us -> 27 us  [on_device(): grad_act, row_total = lax.psum((part_grad, part_loss), 'dp')]
    unnamed x19 -> x18, local copies, waits for them, and re-layouts: 14.5 us -> 14.4 us
  transfers between devices with their start and end apart: 4 -> 5, of which waited for: 3 -> 3; matrix products, arithmetic and copies ran while one was open for 1% -> 3% of each run, Pallas kernels for 0% -> 0%
where the time goes in v1:
time: 551 us; the launch traced here: 550 us
  waiting for transfers between devices  345 us (63%)
  blocking collectives  130 us (24%)
  local copies, waits for them, and re-layouts  20.6 us (4%)
  matrix products  20.6 us (4%)
  starting transfers between devices  18.8 us (3%)
  between operations  14.5 us (3%)
    psum x1, waiting for transfers between devices, on_device(): pre = lax.psum(part_pre, 'dp') + bias_rows  120 us
    all_gather x1, waiting for transfers between devices, on_device(): piece = lax.all_gather(weight, 'latent', axis=1, tiled=True)  114 us
    psum x1, waiting for transfers between devices, on_device(): grad_act, row_total = lax.psum((part_grad, part_loss), 'dp')  111 us
    unnamed x1, blocking collectives  103 us
    psum x1, blocking collectives, on_device(): grad_act, row_total = lax.psum((part_grad, part_loss), 'dp')  27 us
    unnamed x18, local copies, waits for them, and re-layouts  14.4 us
  transfers between devices with their start and end apart: 5, of which 3 were waited for; matrix products, arithmetic and copies ran while one was open for 3% of the time, Pallas kernels for 0%

profile of v1, /device:TPU:1, one launch (start us, length us, event | category | flops | bytes accessed | tf_op | source)
XLA Modules:
  0.0 550.1 jit_solution(3317843526871270815)
XLA Ops:
  7.2 0.0 copy-start
  7.2 0.0 all-gather.2.cloned.1.call-start
  7.2 0.7 all-gather.2.cloned.1.call-update
  7.9 0.0 all-reduce.4.cloned.1.call-start
  8.0 1.3 copy.31
  9.2 113.8 %all-gather.2.cloned.1.call-done = bf16[512,8192]{1,0:T(8,128)(2,1)} async-done(((bf16[512,256]{1,0:T(8,128)(2,1)}), bf16[512,8192]{1,0:T(8,128)(2,1)}) %all-gather.2.cloned.1.call-update) | async-done | bytes 8388624 | tf_op jit(solution)/shard_map/all_gather | solution.py:45
  123.0 0.0 copy-start.5
  123.0 9.3 %copy.53 = bf16[64,8,64,128]{3,2,1,0:T(8,128)(2,1)} copy(bf16[64,8,64,128]{3,1,2,0:T(8,128)(2,1)} %bitcast.54) | data formatting | bytes 16777216
  132.3 0.0 copy-done.5
  132.3 0.0 copy-start.4
  132.3 4.6 convolution_convert_fusion.1
  136.9 0.0 copy-done.4
  137.0 2.1 convolution_bitcast_fusion.1
  139.1 0.0 all-reduce.4.cloned.1.call-update
  139.1 0.0 all-reduce.6.cloned.1.call-start
  139.8 0.0 copy-done
  139.8 0.6 gather_fusion
  140.4 0.1 broadcast_select_fusion
  140.5 120.1 %all-reduce.4.cloned.1.call-done = f32[8,512,128]{1,2,0:T(8,128)} async-done(((f32[8,512,128]{1,2,0:T(8,128)}), f32[8,512,128]{1,2,0:T(8,128)}) %all-reduce.4.cloned.1.call-update) | async-done | bytes 2097168 | tf_op jit(solution)/shard_map/psum | solution.py:57
  260.6 2.5 multiply_reduce_fusion
  263.1 0.0 copy-start.2
  263.1 1.0 copy-done.2
  264.1 2.1 convolution_bitcast_fusion
  266.1 0.0 copy-start.1
  266.1 0.0 all-reduce.6.cloned.1.call-update
  266.2 0.6 stack.2
  266.8 9.3 %all-to-all-start.1 = ((s32[32,1,8]{2,1,0:T(1,128)}), s32[32,1,8]{2,1,0:T(1,128)S(1)}, u32[]{:S(2)}, u32[]{:S(2)}) async-start(s32[32,1,8]{2,1,0:T(1,128)} %stack.2), calls=%async_computation.1 | async-start | bytes 32768 | tf_op jit(solution)/shard_map/all_to_all | solution.py:13
  276.1 110.8 %all-reduce.6.cloned.1.call-done = f32[8,512,128]{1,2,0:T(8,128)} async-done(((f32[8,512,128]{1,2,0:T(8,128)}), f32[8,512,128]{1,2,0:T(8,128)}) %all-reduce.6.cloned.1.call-update) | async-done | bytes 2097168 | tf_op jit(solution)/shard_map/psum | solution.py:64
  386.9 0.0 copy-done.1
  386.9 0.0 copy-start.3
  386.9 2.5 fusion.5
  389.4 0.0 copy-done.3
  389.4 0.8 fusion.2
  390.3 0.8 copy.40
  391.0 1.3 convolution_convert_fusion
  392.4 3.6 copy.41
  396.0 0.0 all-to-all-done.1
  396.0 9.4 %all-to-all-start = ((bf16[32,512,128]{2,1,0:T(8,128)(2,1)}), bf16[32,512,128]{2,1,0:T(8,128)(2,1)}, u32[]{:S(2)}, u32[]{:S(2)}) async-start(bf16[32,512,128]{2,1,0:T(8,128)(2,1)} %copy.41), calls=%async_computation | async-start | bytes 8388608 | tf_op jit(solution)/shard_map/all_to_all | solution.py:73
  405.4 1.3 dynamic-slice
  406.7 0.8 dynamic-update-slice
  407.4 103.0 %all-reduce = s32[32]{0:T(128)S(1)} all-reduce(s32[32]{0:T(128)S(1)} %dynamic-update-slice), channel_id=1, replica_groups=mesh['dp'=16,'latent'=32] {'latent'}, use_global_device_ids=true, to_apply=%add | all-reduce | flops 32 | bytes 256
  510.4 0.1 copy.42
  510.5 0.1 select_reduce_fusion
  510.6 27.0 %psum.23 = f32[512]{0:T(512)S(1)} all-reduce(f32[512]{0:T(512)S(1)} %broadcast_multiply_fusion), channel_id=1, replica_groups=mesh['dp'=16,'latent'=32] {'dp'}, use_global_device_ids=true, to_apply=%region_4.5 | all-reduce | flops 512 | bytes 4096 | tf_op jit(solution)/shard_map/psum | solution.py:64
  537.6 0.6 dynamic_slice.3
  538.2 0.0 all-to-all-done
  538.2 4.6 fusion
  542.8 0.8 copy.66
  (9 shorter events, 0.0 us)
Async XLA Ops:
  7.2 132.7 %copy-start = (f32[8192]{0:T(1024)S(1)}, f32[8192]{0:T(1024)}, u32[]{:S(2)}) copy-start(f32[8192]{0:T(1024)} %param.8) | copy-start | bytes 98308
  7.2 115.8 %all-gather.2.cloned.1.call-start = ((), (), s32[]{:S(2)}) async-start(), calls=%async_computation.2 | async-start | bytes 8650752 | tf_op jit(solution)/shard_map/all_gather | solution.py:45
  7.9 252.7 %all-reduce.4.cloned.1.call-start = ((), (), s32[]{:S(2)}) async-start(), calls=%async_computation.3 | async-start | bytes 4194304 | tf_op jit(solution)/shard_map/psum | solution.py:57
  123.0 9.3 %copy-start.5 = (s32[1,8]{1,0:T(1,128)S(1)}, s32[1,8]{1,0:T(1,128)}, u32[]{:S(2)}) copy-start(s32[1,8]{1,0:T(1,128)} %param.10) | copy-start | bytes 100
  132.3 4.6 copy-start.4
  139.1 247.8 %all-reduce.6.cloned.1.call-start = ((), (), s32[]{:S(2)}) async-start(), calls=%async_computation.4 | async-start | bytes 4194304 | tf_op jit(solution)/shard_map/psum | solution.py:64
  263.1 1.0 copy-start.2
  266.1 120.8 %copy-start.1 = (f32[8,512,128]{1,2,0:T(8,128)S(1)}, f32[8,512,128]{1,2,0:T(8,128)}, u32[]{:S(2)}) copy-start(f32[8,512,128]{1,2,0:T(8,128)} %all-reduce.4.cloned.1.call-done) | copy-start | bytes 6291460
  266.8 129.2 %all-to-all-start.1 = ((s32[32,1,8]{2,1,0:T(1,128)}), s32[32,1,8]{2,1,0:T(1,128)S(1)}, u32[]{:S(2)}, u32[]{:S(2)}) async-start(s32[32,1,8]{2,1,0:T(1,128)} %stack.2), calls=%async_computation.1 | async-start | bytes 32768 | tf_op jit(solution)/shard_map/all_to_all | solution.py:13
  386.9 2.6 copy-start.3
  396.0 142.2 %all-to-all-start = ((bf16[32,512,128]{2,1,0:T(8,128)(2,1)}), bf16[32,512,128]{2,1,0:T(8,128)(2,1)}, u32[]{:S(2)}, u32[]{:S(2)}) async-start(bf16[32,512,128]{2,1,0:T(8,128)(2,1)} %copy.41), calls=%async_computation | async-start | bytes 8388608 | tf_op jit(solution)/shard_map/all_to_all | solution.py:73
Sparse Core Ops, SparseCore 0:
  11.1 111.8 all-gather.1
  139.2 121.3 all-reduce.3
  266.3 120.5 all-reduce.5

commit v2 on v0

--- a/solution.py
+++ b/solution.py
@@ -5,6 +5,7 @@
 from jax.sharding import PartitionSpec as P
 
 BLK = 128
+get_meshes = lambda view, bus_axis: jnp.sum(lax.all_gather(view, bus_axis), axis=0)
 
 
 def on_device(activations, weight, enc_bias, dec_bias, block_ids, counts):
@@ -47,7 +48,7 @@
     tiles = picked.astype(jnp.bfloat16)
     bias_rows = jnp.take(enc_bias.reshape(-1, block), ids, axis=0)[:, None, :]
     part_pre = jnp.einsum("rd,sdk->srk", centered, tiles, preferred_element_type=jnp.float32)
-    pre = lax.psum(part_pre, "dp") + bias_rows
+    pre = get_meshes(part_pre, "dp") + bias_rows
     act = (jnp.maximum(pre, 0.0) * live_cols).astype(jnp.bfloat16)
     recon = jnp.einsum("srk,sdk->rd", act, tiles, preferred_element_type=jnp.float32) + dec_bias
     err = recon - activations.astype(jnp.float32)

time: 584 us -> 654 us (1.12)
  waiting for transfers between devices: 355 us -> 410 us
  other arithmetic: 0.2 us -> 13.2 us
    all_gather x0 -> x1, waiting for transfers between devices: none -> 178 us  [lax.all_gather(view, bus_axis)]
    psum x1 -> x0, waiting for transfers between devices: 120 us -> none  [on_device(): pre = lax.psum(part_pre, 'dp') + bias_rows]
    reduce_sum x0 -> x1, other arithmetic: none -> 13 us  [jnp.sum(lax.all_gather(view, bus_axis), axis=0)]
    unnamed x19 -> x24, local copies, waits for them, and re-layouts: 14.5 us -> 17.2 us
where the time goes in v2:
time: 654 us
  waiting for transfers between devices  410 us (63%)
  blocking collectives  163 us (25%)
  local copies, waits for them, and re-layouts  24.5 us (4%)
  matrix products  18.8 us (3%)
  between operations  14.5 us (2%)
  other arithmetic  13.2 us (2%)
  starting transfers between devices  9.51 us (1%)
    all_gather x1, waiting for transfers between devices, lax.all_gather(view, bus_axis)  178 us
    psum x1, waiting for transfers between devices, on_device(): grad_act, row_total = lax.psum((part_grad, part_loss), 'dp')  119 us
    all_gather x1, blocking collectives, on_device(): lax.all_gather(block_ids, 'latent', axis=0, tiled=True)  116 us
    all_gather x1, waiting for transfers between devices, on_device(): piece = lax.all_gather(weight, 'latent', axis=1, tiled=True)  113 us
    psum x1, blocking collectives, on_device(): grad_act, row_total = lax.psum((part_grad, part_loss), 'dp')  34.4 us
    unnamed x24, local copies, waits for them, and re-layouts  17.2 us
  transfers between devices with their start and end apart: 4, of which 3 were waited for; matrix products, arithmetic and copies ran while one was open for 1% of the time, Pallas kernels for 0%

profile of v2, /device:TPU:1, one launch (start us, length us, event | category | flops | bytes accessed | tf_op | source)
XLA Modules:
  0.0 653.7 jit_solution(8552971366417559309)
XLA Ops:
  7.2 0.0 copy-start
  7.2 0.0 all-gather.5.cloned.1.call-start
  7.2 0.7 all-gather.5.cloned.1.call-update
  7.9 0.0 all-gather.7.cloned.1.call-start
  8.0 2.0 copy.20
  10.0 113.0 %all-gather.5.cloned.1.call-done = bf16[512,8192]{1,0:T(8,128)(2,1)} async-done(((bf16[512,256]{1,0:T(8,128)(2,1)}), bf16[512,8192]{1,0:T(8,128)(2,1)}) %all-gather.5.cloned.1.call-update) | async-done | bytes 8388624 | tf_op jit(solution)/shard_map/all_gather | solution.py:39
  123.0 0.0 copy-start.7
  123.0 9.3 %copy.45 = bf16[64,8,64,128]{3,2,1,0:T(8,128)(2,1)} copy(bf16[64,8,64,128]{3,1,2,0:T(8,128)(2,1)} %bitcast.57) | data formatting | bytes 16777216
  132.3 0.0 copy-done.7
  132.3 0.0 copy-start.2
  132.3 0.0 copy-start.6
  132.3 4.7 convolution_convert_fusion.1
  137.0 0.0 copy-done.2
  137.0 0.0 copy-done.6
  137.0 0.8 convolution_bitcast_fusion.1
  137.8 1.8 copy.23
  139.7 0.0 all-gather.7.cloned.1.call-update
  139.7 0.0 all-reduce.3.cloned.1.call-start
  140.4 0.0 copy-done
  140.4 0.6 gather_fusion
  141.0 0.1 broadcast_select_fusion
  141.1 177.6 %all-gather.7.cloned.1.call-done = f32[128,512,128]{2,1,0:T(8,128)} async-done(((f32[8,512,128]{2,1,0:T(8,128)}), f32[128,512,128]{2,1,0:T(8,128)}) %all-gather.7.cloned.1.call-update) | async-done | bytes 33554448 | tf_op jit(solution)/shard_map/all_gather | solution.py:8
  318.7 13.0 %reduce_sum.27 = f32[8,512,128]{2,1,0:T(8,128)} reduce(f32[16,8,512,128]{3,2,1,0:T(8,128)} %bitcast.55, f32[]{:T(128)} %constant.42.clone.1), dimensions={0}, to_apply=%region_0.0 | reduce | flops 7864320 | bytes 35651588 | tf_op jit(solution)/shard_map/reduce_sum | solution.py:8
  331.7 1.9 copy.44
  333.6 1.9 multiply_reduce_fusion
  335.6 0.0 copy-start.4
  335.6 1.0 copy-done.4
  336.5 2.1 convolution_bitcast_fusion
  338.6 0.0 copy-start.3
  338.6 0.0 all-reduce.3.cloned.1.call-update
  338.6 118.6 %all-reduce.3.cloned.1.call-done = f32[8,512,128]{1,2,0:T(8,128)} async-done(((f32[8,512,128]{1,2,0:T(8,128)}), f32[8,512,128]{1,2,0:T(8,128)}) %all-reduce.3.cloned.1.call-update) | async-done | bytes 2097168 | tf_op jit(solution)/shard_map/psum | solution.py:58
  457.3 0.0 copy-done.3
  457.3 0.0 copy-start.5
  457.3 2.5 fusion.5
  459.8 0.0 copy-done.5
  459.8 0.8 fusion.2
  460.6 0.8 copy.31
  461.4 1.3 convolution_convert_fusion
  462.8 3.6 copy.32
  466.3 9.4 %all-to-all-start = ((bf16[32,512,128]{2,1,0:T(8,128)(2,1)}), bf16[32,512,128]{2,1,0:T(8,128)(2,1)}, u32[]{:S(2)}, u32[]{:S(2)}) async-start(bf16[32,512,128]{2,1,0:T(8,128)(2,1)} %copy.32), calls=%async_computation | async-start | bytes 8388608 | tf_op jit(solution)/shard_map/all_to_all | solution.py:67
  475.8 116.0 %all-gather.1 = s32[32,1,8]{2,1,0:T(1,128)S(1)} all-gather(s32[1,1,8]{2,1,0:T(1,128)S(1)} %bitcast.62), channel_id=1, replica_groups=mesh['dp'=16,'latent'=32] {'latent'}, dimensions={0}, use_global_device_ids=true | all-gather | bytes 1056 | tf_op jit(solution)/shard_map/all_gather | solution.py:20
  591.8 0.1 copy.33
  591.8 1.3 dynamic-slice
  593.1 0.8 dynamic-update-slice
  593.9 12.8 %all-reduce = s32[32]{0:T(128)S(1)} all-reduce(s32[32]{0:T(128)S(1)} %dynamic-update-slice), channel_id=1, replica_groups=mesh['dp'=16,'latent'=32] {'latent'}, use_global_device_ids=true, to_apply=%add | all-reduce | flops 32 | bytes 256
  606.6 0.1 select_reduce_fusion
  606.7 34.4 %psum.15 = f32[512]{0:T(512)S(1)} all-reduce(f32[512]{0:T(512)S(1)} %broadcast_multiply_fusion), channel_id=1, replica_groups=mesh['dp'=16,'latent'=32] {'dp'}, use_global_device_ids=true, to_apply=%region_4.5 | all-reduce | flops 512 | bytes 4096 | tf_op jit(solution)/shard_map/psum | solution.py:58
  641.2 0.0 copy-start.1
  641.2 0.6 dynamic_slice.3
  641.8 0.0 all-to-all-done
  641.8 4.6 fusion
  646.4 0.8 copy.58
  647.2 0.0 copy-done.1
  (9 shorter events, 0.0 us)
Async XLA Ops:
  7.2 133.2 %copy-start = (f32[8192]{0:T(1024)S(1)}, f32[8192]{0:T(1024)}, u32[]{:S(2)}) copy-start(f32[8192]{0:T(1024)} %param.8) | copy-start | bytes 98308
  7.2 115.8 %all-gather.5.cloned.1.call-start = ((), (), s32[]{:S(2)}) async-start(), calls=%async_computation.1 | async-start | bytes 8650752 | tf_op jit(solution)/shard_map/all_gather | solution.py:39
  7.9 310.7 %all-gather.7.cloned.1.call-start = ((), (), s32[]{:S(2)}) async-start(), calls=%async_computation.3 | async-start | bytes 35651584 | tf_op jit(solution)/shard_map/all_gather | solution.py:8
  123.0 9.3 %copy-start.7 = (s32[1,8]{1,0:T(1,128)S(1)}, s32[1,8]{1,0:T(1,128)}, u32[]{:S(2)}) copy-start(s32[1,8]{1,0:T(1,128)} %param.10) | copy-start | bytes 100
  132.3 4.7 copy-start.2
  132.3 4.7 copy-start.6
  139.7 317.6 %all-reduce.3.cloned.1.call-start = ((), (), s32[]{:S(2)}) async-start(), calls=%async_computation.2 | async-start | bytes 4194304 | tf_op jit(solution)/shard_map/psum | solution.py:58
  335.6 1.0 copy-start.4
  338.6 118.7 %copy-start.3 = (bf16[512,512]{0,1:T(8,128)(2,1)S(1)}, bf16[512,512]{0,1:T(8,128)(2,1)}, u32[]{:S(2)}) copy-start(bf16[512,512]{0,1:T(8,128)(2,1)} %copy.20) | copy-start | bytes 1572868
  457.3 2.6 copy-start.5
  466.3 175.4 %all-to-all-start = ((bf16[32,512,128]{2,1,0:T(8,128)(2,1)}), bf16[32,512,128]{2,1,0:T(8,128)(2,1)}, u32[]{:S(2)}, u32[]{:S(2)}) async-start(bf16[32,512,128]{2,1,0:T(8,128)(2,1)} %copy.32), calls=%async_computation | async-start | bytes 8388608 | tf_op jit(solution)/shard_map/all_to_all | solution.py:67
  641.2 6.0 copy-start.1
Sparse Core Ops, SparseCore 0:
  11.1 111.8 all-gather.4
  139.8 178.8 all-gather.6
  338.8 118.4 all-reduce.2
